TPU v7x, 256 devices: a whole 4x4x8 slice. The times are simulated.
256 devices in a mesh: dp: 32 (over x, y, core), seq: 8 (over z).
Axes of the slice: x: 4, y: 4, z: 8, core: 2. Of those that a mesh axis runs over, the one named last changes fastest.
Arguments:
- queries: bfloat16 [64, 1024, 2048], P('dp', 'seq'), may hold values from -10 to 10
- key_states: bfloat16 [64, 1024, 512], P('dp', 'seq'), may hold values from -10 to 10
- value_states: bfloat16 [64, 1024, 512], P('dp', 'seq'), may hold values from -6 to 6
- grad_out: bfloat16 [64, 1024, 2048], P('dp', None, 'seq'), may hold values from -6 to 6
- doc_ids: int32 [64, 1024], replicated, may hold values from 0 to 2, never falling along the last dimension, each value on 1 to 768 neighbouring positions
- partner: int32 [32], replicated, may hold values from 0 to 31, as said below
- swap_rows: int32 [32, 1], replicated, may hold values from 0 to 1, as said below
Outputs:
- attended: bfloat16 [64, 1024, 2048], P('dp', None, 'seq')
- grad_queries: bfloat16 [64, 1024, 2048], P('dp', 'seq')
- grad_keys: bfloat16 [64, 1024, 512], P('dp', 'seq')
- grad_values: bfloat16 [64, 1024, 512], P('dp', 'seq')
Inputs may be any that keep to these rules, and one draw needn't show every extreme that they name: partner[partner[g]] == g and partner[g] != g. `swap_rows`: the 1 entries of one group are distinct.
All inputs are finite; a program needn't handle non-finite values.
Results may differ from a plain program's by a relative error of at most 0.0075.
Values may be sent and summed in bfloat16 or wider, within the bound.
No kernel may reach another device: no remote copies, remote signals or barrier semaphores. Data moves between devices by JAX's collectives and lax.ppermute only.
A program may use at most 64 MiB of HBM per device.

v0:
```python
import functools

import jax
import jax.numpy as jnp
from jax import lax
from jax.experimental import pallas as pl
from jax.experimental.pallas import tpu as pltpu
from jax.sharding import PartitionSpec as P

QH = 16
KVH = 4
HD = 128
BLOCK = 256
FAR = -1e30
ORDER_IN = (1, 7, 4, 3, 5, 2, 6)
ORDER_OUT = (3, 5, 2, 6, 4, 1, 7)
ANY = pl.BlockSpec(memory_space=pl.ANY)
HBM = pl.BlockSpec(memory_space=pltpu.HBM)
SMEM = pl.BlockSpec(memory_space=pltpu.SMEM)
MIB = 1024 * 1024
BF16 = jnp.bfloat16


def dot(a, b, dims=((1,), (0,))):
    return lax.dot_general(a, b, (dims, ((), ())), preferred_element_type=jnp.float32)


def part(index, size):
    return pl.ds(pl.multiple_of(index * size, size), size)


def places(swap_rows):
    moving = swap_rows[0, lax.axis_index("dp")]
    return lax.axis_index("seq"), 1 - moving, moving


class Copies:
    def __init__(self, sems):
        self.sems, self.all = sems, []

    def start(self, source, target):
        copy = pltpu.make_async_copy(source, target, self.sems.at[len(self.all)])
        copy.start()
        self.all.append(copy)
        return copy

    def wait(self, begin=0, end=None):
        for copy in self.all[begin:end]:
            copy.wait()


def call(kernel, operands, outs, scratch, name, aliases=None, limit=60, flops=0, nbytes=2 * MIB):
    return pl.pallas_call(
        kernel,
        out_shape=outs,
        in_specs=[SMEM] + [HBM] * (len(operands) - 1),
        out_specs=[HBM] * len(outs),
        scratch_shapes=scratch,
        input_output_aliases=aliases or {},
        compiler_params=pltpu.CompilerParams(vmem_limit_bytes=limit * MIB),
        cost_estimate=pl.CostEstimate(flops=flops, bytes_accessed=nbytes, transcendentals=0),
        name=name,
    )(*operands)


def pack_kernel(seq, where, q_ref, k_ref, v_ref, grad_ref, *refs):
    outs, grad_out, (chunks, grad, sems_in, sems_out) = refs[:seq], refs[seq], refs[-4:]
    me, *rows = places(where)
    loads, stores = Copies(sems_in), Copies(sems_out)
    order = (*ORDER_IN, 0)
    for s in order:
        to = lax.rem(me + s, seq)
        head, chunk = part(to // 2, HD), chunks.at[s]
        loads.start(q_ref.at[:, :, part(to, 256)], chunk.at[:, :, pl.ds(0, 256)])
        loads.start(k_ref.at[:, :, head], chunk.at[:, :, pl.ds(256, HD)])
        loads.start(v_ref.at[:, :, head], chunk.at[:, :, pl.ds(384, HD)])
        if s == order[0]:
            loads.start(grad_ref.at[rows[1]], grad)
    at = 0
    for s in order:
        loads.wait(at, at + 3)
        stores.start(chunks.at[s], outs[s])
        at += 3
        if s == order[0]:
            loads.wait(at, at + 1)
            stores.start(grad, grad_out)
            at += 1
    stores.wait()


def pack(where, q, k, v, grad, seq):
    tok, length = q.shape[1], grad.shape[1]
    out = call(
        functools.partial(pack_kernel, seq),
        (where, q, k, v, grad),
        [jax.ShapeDtypeStruct((2, tok, 512), BF16)] * seq
        + [jax.ShapeDtypeStruct((length, 256), BF16)],
        [
            pltpu.VMEM((seq, 2, tok, 512), BF16),
            pltpu.VMEM((length, 256), BF16),
            pltpu.SemaphoreType.DMA((3 * seq + 1,)),
            pltpu.SemaphoreType.DMA((seq + 1,)),
        ],
        "pack",
    )
    return out[:seq], out[seq]


def rows_kernel(seq, tok, where, *refs):
    xs, refs = dict(zip((0, *ORDER_IN), refs)), refs[seq:]
    grad_whole, grad_row, marks, att_whole, att_row = refs[0], refs[1], refs[2:6], refs[6], refs[7]
    gs, refs = refs[8 : 8 + seq], refs[8 + seq :]
    x_s, ka, qm, do, kt, vt, dk, dv, att, grads, sems_in, sems_out = refs
    me, *rows_at = places(where)
    length = seq * tok
    steps = length // BLOCK
    per = BLOCK // tok
    scaling = float(HD) ** (-0.5)
    to_log2 = scaling * 1.4426950408889634
    grad_refs = grad_whole.at[rows_at[0]], grad_row
    att_refs = att_whole.at[rows_at[0]], att_row

    def chunk_copy(unit, s, origin):
        return pltpu.make_async_copy(
            xs[s].at[rows_at[unit]], x_s.at[unit, part(origin, tok)], sems_in.at[unit, origin]
        )

    def whole_copies(unit):
        every = [
            (marks[2 * unit], qm.at[unit]),
            (marks[2 * unit + 1], ka.at[unit, :, pl.ds(HD, HD)]),
            (grad_refs[unit], do.at[unit]),
        ]
        return [
            pltpu.make_async_copy(source, target, sems_in.at[unit, seq + n])
            for n, (source, target) in enumerate(every)
        ]

    for unit in range(2):
        for copy in whole_copies(unit):
            copy.start()
        for s in range(seq):
            chunk_copy(unit, s, lax.rem(me + seq - s, seq)).start()
    key_at = lax.broadcasted_iota(jnp.int32, (BLOCK, BLOCK), 0)
    query_at = lax.broadcasted_iota(jnp.int32, (BLOCK, BLOCK), 1)
    causal = key_at <= query_at
    stores = Copies(sems_out)
    for unit, i in [(unit, i) for unit in range(2) for i in range(steps)]:
        rows = slice(i * BLOCK, (i + 1) * BLOCK)
        keys = [slice(b * BLOCK, (b + 1) * BLOCK) for b in range(i + 1)]
        if i == 0:
            for copy in whole_copies(unit):
                copy.wait()
        for origin in range(i * per, (i + 1) * per):
            chunk_copy(unit, 0, origin).wait()
        ka[unit, rows, 0:HD] = x_s[unit, rows, 256:384]
        kt[unit, :, rows] = x_s[unit, rows, 256:384].T
        vt[unit, :, rows] = x_s[unit, rows, 384:512].T
        mark = qm[unit, rows, :]
        plain = [x_s[unit, rows, h * HD : (h + 1) * HD] for h in range(2)]
        queries = [jnp.concatenate([query, mark], axis=1) for query in plain]
        gradients = [do[unit, rows, h * HD : (h + 1) * HD] for h in range(2)]
        scores, grad_probs = [], []
        for h in range(2):
            blocks = [dot(ka[unit, key, :], queries[h], ((1,), (1,))) for key in keys]
            blocks[i] = jnp.where(causal, blocks[i], FAR)
            scores.append(blocks)
        for h in range(2):
            grad_t = gradients[h].T
            grad_probs.append([dot(x_s[unit, key, 384:512], grad_t) for key in keys])
        all_probs, all_dscore = [], []
        for h in range(2):
            cols = slice(h * HD, (h + 1) * HD)
            top = functools.reduce(
                jnp.maximum, [jnp.max(block, axis=0, keepdims=True) for block in scores[h]]
            )
            expo = [jnp.exp2((block - top) * to_log2) for block in scores[h]]
            total = sum(jnp.sum(block, axis=0, keepdims=True) for block in expo)
            inverse = 1.0 / total
            weights = [block * inverse for block in expo]
            probs = [block.astype(BF16) for block in weights]
            out_t = sum(dot(vt[unit, :, key], probs[b]) for b, key in enumerate(keys))
            att[unit, rows, cols] = out_t.T.astype(BF16)
            grad_t = gradients[h].T.astype(jnp.float32)
            inner = jnp.sum(grad_t * out_t, axis=0, keepdims=True)
            dscore = [
                (weights[b] * (grad_probs[h][b] - inner)).astype(BF16) for b in range(i + 1)
            ]
            dq_t = sum(dot(kt[unit, :, key], dscore[b]) for b, key in enumerate(keys))
            grads[unit, rows, cols] = (dq_t * scaling).T.astype(BF16)
            all_probs.append(probs)
            all_dscore.append(dscore)
        both_q = jnp.concatenate(plain, axis=0)
        both_grad = jnp.concatenate(gradients, axis=0)
        for b, key in enumerate(keys):
            more_k = dot(jnp.concatenate([part_[b] for part_ in all_dscore], axis=1), both_q)
            more_v = dot(jnp.concatenate([part_[b] for part_ in all_probs], axis=1), both_grad)
            dk[unit, key, :] = more_k if b == i else dk[unit, key, :] + more_k
            dv[unit, key, :] = more_v if b == i else dv[unit, key, :] + more_v
        at = pl.ds(i * BLOCK, BLOCK)
        stores.start(att.at[unit, at], att_refs[unit].at[at])
        if i == steps - 1:
            grads[unit, :, 256:384] = (dk[unit] * scaling).astype(BF16)
            grads[unit, :, 384:512] = dv[unit].astype(BF16)
            for s in range(seq):
                to = part(lax.rem(me + s, seq), tok)
                stores.start(grads.at[unit, to], gs[s].at[rows_at[unit]])
    stores.wait()


def rows_call(where, xs, grad_whole, grad_row, marks, seq):
    tok = xs[0].shape[1]
    length = seq * tok
    f32 = jnp.float32
    out = call(
        functools.partial(rows_kernel, seq, tok),
        (where, *[xs[s] for s in (0, *ORDER_IN)], grad_whole, grad_row, *marks),
        [
            jax.ShapeDtypeStruct((2, length, 256), BF16),
            jax.ShapeDtypeStruct((length, 256), BF16),
        ]
        + [jax.ShapeDtypeStruct((2, tok, 512), BF16)] * seq,
        [
            pltpu.VMEM((2, length, 512), BF16),
            pltpu.VMEM((2, length, 256), BF16),
            pltpu.VMEM((2, length, HD), BF16),
            pltpu.VMEM((2, length, 256), BF16),
            pltpu.VMEM((2, HD, length), BF16),
            pltpu.VMEM((2, HD, length), BF16),
            pltpu.VMEM((2, length, HD), f32),
            pltpu.VMEM((2, length, HD), f32),
            pltpu.VMEM((2, length, 256), BF16),
            pltpu.VMEM((2, length, 512), BF16),
            pltpu.SemaphoreType.DMA((2, seq + 3)),
            pltpu.SemaphoreType.DMA((2 * (seq + length // BLOCK),)),
        ],
        "rows",
        flops=2 * 10**10,
        nbytes=MIB,
    )
    return out[0], out[1], out[2:]


def unpack_kernel(seq, where, *refs):
    parts = dict(zip((0, *ORDER_OUT), refs))
    row_ref, refs = refs[seq], refs[seq + 2 :]
    att, gq, gk, gv, near, wide, sums, held, sems_in, sems_out = refs
    me, *rows = places(where)
    loads, stores = Copies(sems_in), Copies(sems_out)
    for s in range(seq):
        origin = lax.rem(me + seq - s, seq)
        loads.start(parts[s].at[:, :, pl.ds(256, 256)], near.at[origin])
    for s in range(seq):
        origin = lax.rem(me + seq - s, seq)
        loads.start(parts[s].at[:, :, pl.ds(0, 256)], wide.at[:, :, part(origin, 256)])
    loads.start(row_ref, held)
    loads.wait(0, seq)
    for head in range(KVH):
        both = near[2 * head].astype(jnp.float32) + near[2 * head + 1].astype(jnp.float32)
        both = both.astype(BF16)
        cols = slice(head * HD, (head + 1) * HD)
        sums[0, :, :, cols] = both[:, :, 0:HD]
        sums[1, :, :, cols] = both[:, :, HD:]
    stores.start(sums.at[0], gk)
    stores.start(sums.at[1], gv)
    loads.wait(seq)
    stores.start(wide, gq)
    stores.start(held, att.at[rows[1]])
    stores.wait()


def unpack(where, parts, row, attended, seq):
    tok = parts[0].shape[1]
    return call(
        functools.partial(unpack_kernel, seq),
        (where, *[parts[s] for s in (0, *ORDER_OUT)], row, attended),
        [
            jax.ShapeDtypeStruct(attended.shape, BF16),
            jax.ShapeDtypeStruct((2, tok, QH * HD), BF16),
            jax.ShapeDtypeStruct((2, tok, KVH * HD), BF16),
            jax.ShapeDtypeStruct((2, tok, KVH * HD), BF16),
        ],
        [
            pltpu.VMEM((seq, 2, tok, 256), BF16),
            pltpu.VMEM((2, tok, QH * HD), BF16),
            pltpu.VMEM((2, 2, tok, KVH * HD), BF16),
            pltpu.VMEM(row.shape, BF16),
            pltpu.SemaphoreType.DMA((2 * seq + 1,)),
            pltpu.SemaphoreType.DMA((4,)),
        ],
        "unpack",
        limit=16,
        aliases={2 + seq: 0},
    )


def route_kernel(groups, partner, spread, *refs):
    routed, held, sems = refs[-3:]
    copies = Copies(sems)
    for group in range(groups):
        copies.start(spread.at[partner[group]], held.at[group])
    copies.wait()
    copies.start(held, routed).wait()


def route(partner, spread, after=()):
    groups = spread.shape[0]
    return call(
        functools.partial(route_kernel, groups),
        (partner, spread, *after),
        [jax.ShapeDtypeStruct(spread.shape, spread.dtype)],
        [pltpu.VMEM(spread.shape, spread.dtype), pltpu.SemaphoreType.DMA((groups + 1,))],
        "route",
        limit=8,
    )[0]


def shifted(arrays, seq, order):
    out = {0: arrays[0]}
    for s in order:
        out[s] = lax.ppermute(arrays[s], "seq", [(d, (d + s) % seq) for d in range(seq)])
    return [out[s] for s in range(seq)], tuple(out[s] for s in order)


def swapped(row, partner, after=()):
    groups = lax.axis_size("dp")
    shape = row.shape
    pieces = row.reshape(groups, shape[0] // groups, shape[1])
    spread = lax.all_to_all(pieces, "dp", 0, 0, tiled=True)
    routed = route(partner, spread, after)
    return lax.all_to_all(routed, "dp", 0, 0, tiled=True).reshape(shape)


def per_device(queries, key_states, value_states, grad_out, doc_ids, partner, swap_rows):
    seq = lax.axis_size("seq")
    group = lax.axis_index("dp")
    moving = swap_rows[group, 0]
    staying = 1 - moving
    where = swap_rows.reshape(1, -1)
    docs = lax.dynamic_slice_in_dim(doc_ids, group * 2, 2, 0)
    lanes = jnp.arange(HD, dtype=jnp.int32)

    def marks(row):
        same = lax.dynamic_index_in_dim(docs, row, 0, False)[:, None] == lanes
        return jnp.where(same, 0.0, FAR).astype(BF16), same.astype(BF16)

    sent, grad_row = pack(where, queries, key_states, value_states, grad_out, seq)
    got, _ = shifted(sent, seq, ORDER_IN)
    grad_move = swapped(grad_row, partner)
    attended, att_move, back = rows_call(
        where, got, grad_out, grad_move, (*marks(staying), *marks(moving)), seq
    )
    returned, early = shifted(back, seq, ORDER_OUT)
    att_move = swapped(att_move, partner)
    return unpack(where, returned, att_move, attended, seq)


def solution(mesh):
    return jax.shard_map(
        per_device,
        mesh=mesh,
        in_specs=(
            P("dp", "seq", None),
            P("dp", "seq", None),
            P("dp", "seq", None),
            P("dp", None, "seq"),
            P(),
            P(),
            P(),
        ),
        out_specs=(
            P("dp", None, "seq"),
            P("dp", "seq", None),
            P("dp", "seq", None),
            P("dp", "seq", None),
        ),
        check_vma=False,
    )
```

profile of v0, /device:TPU:1, one launch (start us, length us, event | category | flops | bytes accessed | tf_op | source)
XLA Modules:
  0.0 145.5 jit_solution(13781538895544387380)
XLA Ops:
  0.6 3.6 %pack.1 = (bf16[2,128,512]{2,1,0:T(8,128)(2,1)}, bf16[2,128,512]{2,1,0:T(8,128)(2,1)}, bf16[2,128,512]{2,1,0:T(8,128)(2,1)}, bf16[2,128,512]{2,1,0:T(8,128)(2,1)...) custom-call(s32[1,32]{1,0:T(1,128)} %bitcast.9, ...), custom_call_target="tpu_custom_call" | custom-call | bytes 2097152 | tf_op jit(solution)/shard_map/pack/pallas_call | solution.py:53
  4.2 8.7 %all-to-all-start = ((bf16[32,32,256]{2,1,0:T(8,128)(2,1)}), bf16[32,32,256]{2,1,0:T(8,128)(2,1)S(1)}, u32[]{:S(2)}, u32[]{:S(2)}) async-start(bf16[32,32,256]{2,1,0:T(8,128)(2,1)} %bitcast.12), calls=%async_computation | async-start | bytes 1048576 | tf_op jit(solution)/shard_map/all_to_all | solution.py:329
  13.0 1.7 %collective-permute-start = (bf16[2,128,512]{2,1,0:T(8,128)(2,1)}, bf16[2,128,512]{2,1,0:T(8,128)(2,1)S(1)}, u32[]{:S(2)}, u32[]{:S(2)}) collective-permute-start(bf16[2,128,512]{2,1,0:T(8,128)(2,1)} %get-tuple-element.24), channel_id=1, source_target_pairs={{0,1},{1,2},{2,3},{3,4},{4,5},{5,6},{6,7},{7,0},{8,9},{9,10},{10,1... | collective-permute-start | bytes 786440 | tf_op jit(solution)/shard_map/ppermute | solution.py:321
  14.7 4.0 %collective-permute-start.1 = (bf16[2,128,512]{2,1,0:T(8,128)(2,1)S(1)}, bf16[2,128,512]{2,1,0:T(8,128)(2,1)S(1)}, u32[]{:S(2)}, u32[]{:S(2)}) collective-permute-start(bf16[2,128,512]{2,1,0:T(8,128)(2,1)S(1)} %copy-done.15), channel_id=1, source_target_pairs={{0,7},{1,0},{2,1},{3,2},{4,3},{5,4},{6,5},{7,6},{8,15},{9,8},{10,9... | collective-permute-start | bytes 786440 | tf_op jit(solution)/shard_map/ppermute | solution.py:321
  18.7 3.9 %collective-permute-start.2 = (bf16[2,128,512]{2,1,0:T(8,128)(2,1)S(1)}, bf16[2,128,512]{2,1,0:T(8,128)(2,1)S(1)}, u32[]{:S(2)}, u32[]{:S(2)}) collective-permute-start(bf16[2,128,512]{2,1,0:T(8,128)(2,1)S(1)} %copy-done.14), channel_id=1, source_target_pairs={{0,4},{1,5},{2,6},{3,7},{4,0},{5,1},{6,2},{7,3},{8,12},{9,13},{10,... | collective-permute-start | bytes 786440 | tf_op jit(solution)/shard_map/ppermute | solution.py:321
  23.1 4.0 %collective-permute-start.4 = (bf16[2,128,512]{2,1,0:T(8,128)(2,1)S(1)}, bf16[2,128,512]{2,1,0:T(8,128)(2,1)S(1)}, u32[]{:S(2)}, u32[]{:S(2)}) collective-permute-start(bf16[2,128,512]{2,1,0:T(8,128)(2,1)S(1)} %copy-done.12), channel_id=1, source_target_pairs={{0,5},{1,6},{2,7},{3,0},{4,1},{5,2},{6,3},{7,4},{8,13},{9,14},{10,... | collective-permute-start | bytes 786440 | tf_op jit(solution)/shard_map/ppermute | solution.py:321
  32.2 2.5 %route.2 = bf16[32,32,256]{2,1,0:T(8,128)(2,1)} custom-call(s32[32]{0:T(128)S(1)} %copy-done.1, bf16[32,32,256]{2,1,0:T(8,128)(2,1)S(1)} %all-to-all-done.spread), custom_call_target="tpu_custom_call" | custom-call | bytes 2097152 | tf_op jit(solution)/shard_map/route/pallas_call | solution.py:53
  34.7 8.9 %all-to-all-start.1 = ((bf16[32,32,256]{2,1,0:T(8,128)(2,1)}), bf16[32,32,256]{2,1,0:T(8,128)(2,1)S(1)}, u32[]{:S(2)}, u32[]{:S(2)}) async-start(bf16[32,32,256]{2,1,0:T(8,128)(2,1)} %route.2), calls=%async_computation.1 | async-start | bytes 1048576 | tf_op jit(solution)/shard_map/all_to_all | solution.py:331
  43.7 0.9 constant_dynamic-slice_fusion
  44.7 3.8 %collective-permute-start.6 = (bf16[2,128,512]{2,1,0:T(8,128)(2,1)S(1)}, bf16[2,128,512]{2,1,0:T(8,128)(2,1)S(1)}, u32[]{:S(2)}, u32[]{:S(2)}) collective-permute-start(bf16[2,128,512]{2,1,0:T(8,128)(2,1)S(1)} %copy-done.10), channel_id=1, source_target_pairs={{0,6},{1,7},{2,0},{3,1},{4,2},{5,3},{6,4},{7,5},{8,14},{9,15},{10,... | collective-permute-start | bytes 786440 | tf_op jit(solution)/shard_map/ppermute | solution.py:321
  48.5 1.1 fusion
  49.6 1.1 select_convert_fusion
  50.8 1.7 %collective-permute-done.3.refs_4_ = bf16[2,128,512]{2,1,0:T(8,128)(2,1)S(1)} collective-permute-done((bf16[2,128,512]{2,1,0:T(8,128)(2,1)S(1)}, bf16[2,128,512]{2,1,0:T(8,128)(2,1)S(1)}, u32[]{:S(2)}, u32[]{:S(2)}) %collective-permute-start.3) | collective-permute-done | bytes 262176 | tf_op jit(solution)/shard_map/ppermute | solution.py:321
  52.5 5.3 %collective-permute-done.4.refs_5_ = bf16[2,128,512]{2,1,0:T(8,128)(2,1)S(1)} collective-permute-done((bf16[2,128,512]{2,1,0:T(8,128)(2,1)S(1)}, bf16[2,128,512]{2,1,0:T(8,128)(2,1)S(1)}, u32[]{:S(2)}, u32[]{:S(2)}) %collective-permute-start.4) | collective-permute-done | bytes 262176 | tf_op jit(solution)/shard_map/ppermute | solution.py:321
  57.8 2.5 %collective-permute-done.5.refs_6_ = bf16[2,128,512]{2,1,0:T(8,128)(2,1)S(1)} collective-permute-done((bf16[2,128,512]{2,1,0:T(8,128)(2,1)S(1)}, bf16[2,128,512]{2,1,0:T(8,128)(2,1)S(1)}, u32[]{:S(2)}, u32[]{:S(2)}) %collective-permute-start.5) | collective-permute-done | bytes 262176 | tf_op jit(solution)/shard_map/ppermute | solution.py:321
  61.0 5.4 %collective-permute-done.6.refs_7_ = bf16[2,128,512]{2,1,0:T(8,128)(2,1)S(1)} collective-permute-done((bf16[2,128,512]{2,1,0:T(8,128)(2,1)S(1)}, bf16[2,128,512]{2,1,0:T(8,128)(2,1)S(1)}, u32[]{:S(2)}, u32[]{:S(2)}) %collective-permute-start.6) | collective-permute-done | bytes 262176 | tf_op jit(solution)/shard_map/ppermute | solution.py:321
  67.2 16.3 %rows.1 = (bf16[2,1024,256]{2,1,0:T(8,128)(2,1)}, bf16[1024,256]{1,0:T(8,128)(2,1)}, bf16[2,128,512]{2,1,0:T(8,128)(2,1)}, bf16[2,128,512]{2,1,0:T(8,128)(2,1)},...) custom-call(s32[1,32]{1,0:T(1,128)} %bitcast.10, ...), custom_call_target="tpu_custom_call" | custom-call | flops 20000000000 | bytes 1048576 | tf_op jit(solution)/shard_map/rows/pallas_call | solution.py:53
  83.5 7.6 %all-to-all-start.2 = ((bf16[32,32,256]{2,1,0:T(8,128)(2,1)}), bf16[32,32,256]{2,1,0:T(8,128)(2,1)S(1)}, u32[]{:S(2)}, u32[]{:S(2)}) async-start(bf16[32,32,256]{2,1,0:T(8,128)(2,1)} %bitcast.14), calls=%async_computation.2 | async-start | bytes 1048576 | tf_op jit(solution)/shard_map/all_to_all | solution.py:329
  91.2 0.8 collective-permute-start.7
  92.0 3.8 %collective-permute-start.8 = (bf16[2,128,512]{2,1,0:T(8,128)(2,1)S(1)}, bf16[2,128,512]{2,1,0:T(8,128)(2,1)S(1)}, u32[]{:S(2)}, u32[]{:S(2)}) collective-permute-start(bf16[2,128,512]{2,1,0:T(8,128)(2,1)S(1)} %copy-done.19), channel_id=1, source_target_pairs={{0,5},{1,6},{2,7},{3,0},{4,1},{5,2},{6,3},{7,4},{8,13},{9,14},{10,... | collective-permute-start | bytes 786440 | tf_op jit(solution)/shard_map/ppermute | solution.py:321
  95.7 7.1 %all-to-all-done.2.spread = bf16[32,32,256]{2,1,0:T(8,128)(2,1)S(1)} async-done(((bf16[32,32,256]{2,1,0:T(8,128)(2,1)}), bf16[32,32,256]{2,1,0:T(8,128)(2,1)S(1)}, u32[]{:S(2)}, u32[]{:S(2)}) %all-to-all-start.2) | async-done | bytes 524320 | tf_op jit(solution)/shard_map/all_to_all | solution.py:329
  102.8 2.5 %route.3 = bf16[32,32,256]{2,1,0:T(8,128)(2,1)} custom-call(s32[32]{0:T(128)S(1)} %copy-done.1, bf16[32,32,256]{2,1,0:T(8,128)(2,1)S(1)} %all-to-all-done.2.spread), custom_call_target="tpu_custom_call" | custom-call | bytes 2097152 | tf_op jit(solution)/shard_map/route/pallas_call | solution.py:53
  105.3 3.8 %all-to-all-start.3 = ((bf16[32,32,256]{2,1,0:T(8,128)(2,1)}), bf16[32,32,256]{2,1,0:T(8,128)(2,1)S(1)}, u32[]{:S(2)}, u32[]{:S(2)}) async-start(bf16[32,32,256]{2,1,0:T(8,128)(2,1)} %route.3), calls=%async_computation.3 | async-start | bytes 1048576 | tf_op jit(solution)/shard_map/all_to_all | solution.py:331
  109.1 2.5 %collective-permute-start.9 = (bf16[2,128,512]{2,1,0:T(8,128)(2,1)}, bf16[2,128,512]{2,1,0:T(8,128)(2,1)S(1)}, u32[]{:S(2)}, u32[]{:S(2)}) collective-permute-start(bf16[2,128,512]{2,1,0:T(8,128)(2,1)} %get-tuple-element.35), channel_id=1, source_target_pairs={{0,2},{1,3},{2,4},{3,5},{4,6},{5,7},{6,0},{7,1},{8,10},{9,11},{10,... | collective-permute-start | bytes 786440 | tf_op jit(solution)/shard_map/ppermute | solution.py:321
  111.7 1.1 collective-permute-start.10
  112.8 2.3 %collective-permute-start.11 = (bf16[2,128,512]{2,1,0:T(8,128)(2,1)S(1)}, bf16[2,128,512]{2,1,0:T(8,128)(2,1)S(1)}, u32[]{:S(2)}, u32[]{:S(2)}) collective-permute-start(bf16[2,128,512]{2,1,0:T(8,128)(2,1)S(1)} %copy-done.18), channel_id=1, source_target_pairs={{0,4},{1,5},{2,6},{3,7},{4,0},{5,1},{6,2},{7,3},{8,12},{9,13},{10,... | collective-permute-start | bytes 786440 | tf_op jit(solution)/shard_map/ppermute | solution.py:321
  115.1 2.2 %collective-permute-start.12 = (bf16[2,128,512]{2,1,0:T(8,128)(2,1)S(1)}, bf16[2,128,512]{2,1,0:T(8,128)(2,1)S(1)}, u32[]{:S(2)}, u32[]{:S(2)}) collective-permute-start(bf16[2,128,512]{2,1,0:T(8,128)(2,1)S(1)} %copy-done.17), channel_id=1, source_target_pairs={{0,1},{1,2},{2,3},{3,4},{4,5},{5,6},{6,7},{7,0},{8,9},{9,10},{10,1... | collective-permute-start | bytes 786440 | tf_op jit(solution)/shard_map/ppermute | solution.py:321
  117.8 6.9 %collective-permute-done.9.refs_3_ = bf16[2,128,512]{2,1,0:T(8,128)(2,1)S(1)} collective-permute-done((bf16[2,128,512]{2,1,0:T(8,128)(2,1)}, bf16[2,128,512]{2,1,0:T(8,128)(2,1)S(1)}, u32[]{:S(2)}, u32[]{:S(2)}) %collective-permute-start.9) | collective-permute-done | bytes 262176 | tf_op jit(solution)/shard_map/ppermute | solution.py:321
  124.6 1.8 %collective-permute-done.10.refs_4_ = bf16[2,128,512]{2,1,0:T(8,128)(2,1)S(1)} collective-permute-done((bf16[2,128,512]{2,1,0:T(8,128)(2,1)}, bf16[2,128,512]{2,1,0:T(8,128)(2,1)S(1)}, u32[]{:S(2)}, u32[]{:S(2)}) %collective-permute-start.10) | collective-permute-done | bytes 262176 | tf_op jit(solution)/shard_map/ppermute | solution.py:321
  126.5 11.6 %collective-permute-done.11.refs_5_ = bf16[2,128,512]{2,1,0:T(8,128)(2,1)S(1)} collective-permute-done((bf16[2,128,512]{2,1,0:T(8,128)(2,1)S(1)}, bf16[2,128,512]{2,1,0:T(8,128)(2,1)S(1)}, u32[]{:S(2)}, u32[]{:S(2)}) %collective-permute-start.11) | collective-permute-done | bytes 262176 | tf_op jit(solution)/shard_map/ppermute | solution.py:321
  138.1 3.3 %collective-permute-done.12.refs_6_ = bf16[2,128,512]{2,1,0:T(8,128)(2,1)S(1)} collective-permute-done((bf16[2,128,512]{2,1,0:T(8,128)(2,1)S(1)}, bf16[2,128,512]{2,1,0:T(8,128)(2,1)S(1)}, u32[]{:S(2)}, u32[]{:S(2)}) %collective-permute-start.12) | collective-permute-done | bytes 262176 | tf_op jit(solution)/shard_map/ppermute | solution.py:321
  142.8 2.5 %unpack.1 = (bf16[2,1024,256]{2,1,0:T(8,128)(2,1)}, bf16[2,128,2048]{2,1,0:T(8,128)(2,1)}, bf16[2,128,512]{2,1,0:T(8,128)(2,1)}, bf16[2,128,512]{2,1,0:T(8,128)(2,1)}) custom-call(s32[1,32]{1,0:T(1,128)S(1)} %bitcast.11, bf16[2,128,512]{2,1,0:T(8,128)(2,1)S(1)} %copy-done, ...), custom_call_target="tpu_custom_call", output_to_operand_aliasing={{0}: (10, {})} | custom-call | bytes 2097152 | tf_op jit(solution)/shard_map/unpack/pallas_call | solution.py:53
  (59 shorter events, 6.0 us)
Async XLA Ops:
  4.2 10.5 %copy-start.15 = (bf16[2,128,512]{2,1,0:T(8,128)(2,1)S(1)}, bf16[2,128,512]{2,1,0:T(8,128)(2,1)}, u32[]{:S(2)}) copy-start(bf16[2,128,512]{2,1,0:T(8,128)(2,1)} %get-tuple-element.25) | copy-start | bytes 786436
  4.2 14.5 %copy-start.14 = (bf16[2,128,512]{2,1,0:T(8,128)(2,1)S(1)}, bf16[2,128,512]{2,1,0:T(8,128)(2,1)}, u32[]{:S(2)}) copy-start(bf16[2,128,512]{2,1,0:T(8,128)(2,1)} %get-tuple-element.26) | copy-start | bytes 786436
  4.2 18.4 %copy-start.13 = (bf16[2,128,512]{2,1,0:T(8,128)(2,1)S(1)}, bf16[2,128,512]{2,1,0:T(8,128)(2,1)}, u32[]{:S(2)}) copy-start(bf16[2,128,512]{2,1,0:T(8,128)(2,1)} %get-tuple-element.27) | copy-start | bytes 786436
  4.2 18.9 %copy-start.12 = (bf16[2,128,512]{2,1,0:T(8,128)(2,1)S(1)}, bf16[2,128,512]{2,1,0:T(8,128)(2,1)}, u32[]{:S(2)}) copy-start(bf16[2,128,512]{2,1,0:T(8,128)(2,1)} %get-tuple-element.28) | copy-start | bytes 786436
  4.2 27.4 %all-to-all-start = ((bf16[32,32,256]{2,1,0:T(8,128)(2,1)}), bf16[32,32,256]{2,1,0:T(8,128)(2,1)S(1)}, u32[]{:S(2)}, u32[]{:S(2)}) async-start(bf16[32,32,256]{2,1,0:T(8,128)(2,1)} %bitcast.12), calls=%async_computation | async-start | bytes 1048576 | tf_op jit(solution)/shard_map/all_to_all | solution.py:329
  13.0 31.5 %collective-permute-start = (bf16[2,128,512]{2,1,0:T(8,128)(2,1)}, bf16[2,128,512]{2,1,0:T(8,128)(2,1)S(1)}, u32[]{:S(2)}, u32[]{:S(2)}) collective-permute-start(bf16[2,128,512]{2,1,0:T(8,128)(2,1)} %get-tuple-element.24), channel_id=1, source_target_pairs={{0,1},{1,2},{2,3},{3,4},{4,5},{5,6},{6,7},{7,0},{8,9},{9,10},{10,1... | collective-permute-start | bytes 786440 | tf_op jit(solution)/shard_map/ppermute | solution.py:321
  14.7 30.0 %collective-permute-start.1 = (bf16[2,128,512]{2,1,0:T(8,128)(2,1)S(1)}, bf16[2,128,512]{2,1,0:T(8,128)(2,1)S(1)}, u32[]{:S(2)}, u32[]{:S(2)}) collective-permute-start(bf16[2,128,512]{2,1,0:T(8,128)(2,1)S(1)} %copy-done.15), channel_id=1, source_target_pairs={{0,7},{1,0},{2,1},{3,2},{4,3},{5,4},{6,5},{7,6},{8,15},{9,8},{10,9... | collective-permute-start | bytes 786440 | tf_op jit(solution)/shard_map/ppermute | solution.py:321
  18.7 32.0 %collective-permute-start.2 = (bf16[2,128,512]{2,1,0:T(8,128)(2,1)S(1)}, bf16[2,128,512]{2,1,0:T(8,128)(2,1)S(1)}, u32[]{:S(2)}, u32[]{:S(2)}) collective-permute-start(bf16[2,128,512]{2,1,0:T(8,128)(2,1)S(1)} %copy-done.14), channel_id=1, source_target_pairs={{0,4},{1,5},{2,6},{3,7},{4,0},{5,1},{6,2},{7,3},{8,12},{9,13},{10,... | collective-permute-start | bytes 786440 | tf_op jit(solution)/shard_map/ppermute | solution.py:321
  22.7 29.8 %collective-permute-start.3 = (bf16[2,128,512]{2,1,0:T(8,128)(2,1)S(1)}, bf16[2,128,512]{2,1,0:T(8,128)(2,1)S(1)}, u32[]{:S(2)}, u32[]{:S(2)}) collective-permute-start(bf16[2,128,512]{2,1,0:T(8,128)(2,1)S(1)} %copy-done.13), channel_id=1, source_target_pairs={{0,3},{1,4},{2,5},{3,6},{4,7},{5,0},{6,1},{7,2},{8,11},{9,12},{10,... | collective-permute-start | bytes 786440 | tf_op jit(solution)/shard_map/ppermute | solution.py:321
  23.1 34.7 %collective-permute-start.4 = (bf16[2,128,512]{2,1,0:T(8,128)(2,1)S(1)}, bf16[2,128,512]{2,1,0:T(8,128)(2,1)S(1)}, u32[]{:S(2)}, u32[]{:S(2)}) collective-permute-start(bf16[2,128,512]{2,1,0:T(8,128)(2,1)S(1)} %copy-done.12), channel_id=1, source_target_pairs={{0,5},{1,6},{2,7},{3,0},{4,1},{5,2},{6,3},{7,4},{8,13},{9,14},{10,... | collective-permute-start | bytes 786440 | tf_op jit(solution)/shard_map/ppermute | solution.py:321
  34.7 9.8 %copy-start.11 = (bf16[2,128,512]{2,1,0:T(8,128)(2,1)S(1)}, bf16[2,128,512]{2,1,0:T(8,128)(2,1)}, u32[]{:S(2)}) copy-start(bf16[2,128,512]{2,1,0:T(8,128)(2,1)} %get-tuple-element.29) | copy-start | bytes 786436
  34.7 9.9 %copy-start.10 = (bf16[2,128,512]{2,1,0:T(8,128)(2,1)S(1)}, bf16[2,128,512]{2,1,0:T(8,128)(2,1)}, u32[]{:S(2)}) copy-start(bf16[2,128,512]{2,1,0:T(8,128)(2,1)} %get-tuple-element.30) | copy-start | bytes 786436
  34.7 31.6 %all-to-all-start.1 = ((bf16[32,32,256]{2,1,0:T(8,128)(2,1)}), bf16[32,32,256]{2,1,0:T(8,128)(2,1)S(1)}, u32[]{:S(2)}, u32[]{:S(2)}) async-start(bf16[32,32,256]{2,1,0:T(8,128)(2,1)} %route.2), calls=%async_computation.1 | async-start | bytes 1048576 | tf_op jit(solution)/shard_map/all_to_all | solution.py:331
  44.6 15.7 %collective-permute-start.5 = (bf16[2,128,512]{2,1,0:T(8,128)(2,1)S(1)}, bf16[2,128,512]{2,1,0:T(8,128)(2,1)S(1)}, u32[]{:S(2)}, u32[]{:S(2)}) collective-permute-start(bf16[2,128,512]{2,1,0:T(8,128)(2,1)S(1)} %copy-done.11), channel_id=1, source_target_pairs={{0,2},{1,3},{2,4},{3,5},{4,6},{5,7},{6,0},{7,1},{8,10},{9,11},{10,... | collective-permute-start | bytes 786440 | tf_op jit(solution)/shard_map/ppermute | solution.py:321
  44.7 21.7 %collective-permute-start.6 = (bf16[2,128,512]{2,1,0:T(8,128)(2,1)S(1)}, bf16[2,128,512]{2,1,0:T(8,128)(2,1)S(1)}, u32[]{:S(2)}, u32[]{:S(2)}) collective-permute-start(bf16[2,128,512]{2,1,0:T(8,128)(2,1)S(1)} %copy-done.10), channel_id=1, source_target_pairs={{0,6},{1,7},{2,0},{3,1},{4,2},{5,3},{6,4},{7,5},{8,14},{9,15},{10,... | collective-permute-start | bytes 786440 | tf_op jit(solution)/shard_map/ppermute | solution.py:321
  50.8 15.6 %copy-start.7 = (bf16[2,128,512]{2,1,0:T(8,128)(2,1)}, bf16[2,128,512]{2,1,0:T(8,128)(2,1)S(1)}, u32[]{:S(2)}) copy-start(bf16[2,128,512]{2,1,0:T(8,128)(2,1)S(1)} %collective-permute-done.2.refs_3_) | copy-start | bytes 786436
  52.5 13.9 %copy-start.8 = (bf16[2,128,512]{2,1,0:T(8,128)(2,1)}, bf16[2,128,512]{2,1,0:T(8,128)(2,1)S(1)}, u32[]{:S(2)}) copy-start(bf16[2,128,512]{2,1,0:T(8,128)(2,1)S(1)} %collective-permute-done.3.refs_4_) | copy-start | bytes 786436
  57.8 8.6 %copy-start.9 = (bf16[2,128,512]{2,1,0:T(8,128)(2,1)}, bf16[2,128,512]{2,1,0:T(8,128)(2,1)S(1)}, u32[]{:S(2)}) copy-start(bf16[2,128,512]{2,1,0:T(8,128)(2,1)S(1)} %collective-permute-done.4.refs_5_) | copy-start | bytes 786436
  83.5 7.7 %copy-start.21 = (bf16[2,128,512]{2,1,0:T(8,128)(2,1)S(1)}, bf16[2,128,512]{2,1,0:T(8,128)(2,1)}, u32[]{:S(2)}) copy-start(bf16[2,128,512]{2,1,0:T(8,128)(2,1)} %get-tuple-element.33) | copy-start | bytes 786436
  83.5 8.4 %copy-start.19 = (bf16[2,128,512]{2,1,0:T(8,128)(2,1)S(1)}, bf16[2,128,512]{2,1,0:T(8,128)(2,1)}, u32[]{:S(2)}) copy-start(bf16[2,128,512]{2,1,0:T(8,128)(2,1)} %get-tuple-element.34) | copy-start | bytes 786436
  83.5 19.3 %all-to-all-start.2 = ((bf16[32,32,256]{2,1,0:T(8,128)(2,1)}), bf16[32,32,256]{2,1,0:T(8,128)(2,1)S(1)}, u32[]{:S(2)}, u32[]{:S(2)}) async-start(bf16[32,32,256]{2,1,0:T(8,128)(2,1)} %bitcast.14), calls=%async_computation.2 | async-start | bytes 1048576 | tf_op jit(solution)/shard_map/all_to_all | solution.py:329
  91.2 23.9 %collective-permute-start.7 = (bf16[2,128,512]{2,1,0:T(8,128)(2,1)S(1)}, bf16[2,128,512]{2,1,0:T(8,128)(2,1)S(1)}, u32[]{:S(2)}, u32[]{:S(2)}) collective-permute-start(bf16[2,128,512]{2,1,0:T(8,128)(2,1)S(1)} %copy-done.21), channel_id=1, source_target_pairs={{0,3},{1,4},{2,5},{3,6},{4,7},{5,0},{6,1},{7,2},{8,11},{9,12},{10,... | collective-permute-start | bytes 786440 | tf_op jit(solution)/shard_map/ppermute | solution.py:321
  92.0 25.3 %collective-permute-start.8 = (bf16[2,128,512]{2,1,0:T(8,128)(2,1)S(1)}, bf16[2,128,512]{2,1,0:T(8,128)(2,1)S(1)}, u32[]{:S(2)}, u32[]{:S(2)}) collective-permute-start(bf16[2,128,512]{2,1,0:T(8,128)(2,1)S(1)} %copy-done.19), channel_id=1, source_target_pairs={{0,5},{1,6},{2,7},{3,0},{4,1},{5,2},{6,3},{7,4},{8,13},{9,14},{10,... | collective-permute-start | bytes 786440 | tf_op jit(solution)/shard_map/ppermute | solution.py:321
  105.3 9.8 %copy-start.17 = (bf16[2,128,512]{2,1,0:T(8,128)(2,1)S(1)}, bf16[2,128,512]{2,1,0:T(8,128)(2,1)}, u32[]{:S(2)}) copy-start(bf16[2,128,512]{2,1,0:T(8,128)(2,1)} %get-tuple-element.38) | copy-start | bytes 786436
  105.3 11.9 %copy-start.16 = (bf16[2,128,512]{2,1,0:T(8,128)(2,1)S(1)}, bf16[2,128,512]{2,1,0:T(8,128)(2,1)}, u32[]{:S(2)}) copy-start(bf16[2,128,512]{2,1,0:T(8,128)(2,1)} %get-tuple-element.39) | copy-start | bytes 786436
  105.3 36.9 %copy-start = (bf16[2,128,512]{2,1,0:T(8,128)(2,1)S(1)}, bf16[2,128,512]{2,1,0:T(8,128)(2,1)}, u32[]{:S(2)}) copy-start(bf16[2,128,512]{2,1,0:T(8,128)(2,1)} %get-tuple-element.32.refs_0_) | copy-start | bytes 786436
  105.3 36.9 %all-to-all-start.3 = ((bf16[32,32,256]{2,1,0:T(8,128)(2,1)}), bf16[32,32,256]{2,1,0:T(8,128)(2,1)S(1)}, u32[]{:S(2)}, u32[]{:S(2)}) async-start(bf16[32,32,256]{2,1,0:T(8,128)(2,1)} %route.3), calls=%async_computation.3 | async-start | bytes 1048576 | tf_op jit(solution)/shard_map/all_to_all | solution.py:331
  109.1 15.5 %collective-permute-start.9 = (bf16[2,128,512]{2,1,0:T(8,128)(2,1)}, bf16[2,128,512]{2,1,0:T(8,128)(2,1)S(1)}, u32[]{:S(2)}, u32[]{:S(2)}) collective-permute-start(bf16[2,128,512]{2,1,0:T(8,128)(2,1)} %get-tuple-element.35), channel_id=1, source_target_pairs={{0,2},{1,3},{2,4},{3,5},{4,6},{5,7},{6,0},{7,1},{8,10},{9,11},{10,... | collective-permute-start | bytes 786440 | tf_op jit(solution)/shard_map/ppermute | solution.py:321
  111.7 14.8 %collective-permute-start.10 = (bf16[2,128,512]{2,1,0:T(8,128)(2,1)}, bf16[2,128,512]{2,1,0:T(8,128)(2,1)S(1)}, u32[]{:S(2)}, u32[]{:S(2)}) collective-permute-start(bf16[2,128,512]{2,1,0:T(8,128)(2,1)} %get-tuple-element.36), channel_id=1, source_target_pairs={{0,6},{1,7},{2,0},{3,1},{4,2},{5,3},{6,4},{7,5},{8,14},{9,15},{10,... | collective-permute-start | bytes 786440 | tf_op jit(solution)/shard_map/ppermute | solution.py:321
  112.8 25.3 %collective-permute-start.11 = (bf16[2,128,512]{2,1,0:T(8,128)(2,1)S(1)}, bf16[2,128,512]{2,1,0:T(8,128)(2,1)S(1)}, u32[]{:S(2)}, u32[]{:S(2)}) collective-permute-start(bf16[2,128,512]{2,1,0:T(8,128)(2,1)S(1)} %copy-done.18), channel_id=1, source_target_pairs={{0,4},{1,5},{2,6},{3,7},{4,0},{5,1},{6,2},{7,3},{8,12},{9,13},{10,... | collective-permute-start | bytes 786440 | tf_op jit(solution)/shard_map/ppermute | solution.py:321
  115.1 26.3 %collective-permute-start.12 = (bf16[2,128,512]{2,1,0:T(8,128)(2,1)S(1)}, bf16[2,128,512]{2,1,0:T(8,128)(2,1)S(1)}, u32[]{:S(2)}, u32[]{:S(2)}) collective-permute-start(bf16[2,128,512]{2,1,0:T(8,128)(2,1)S(1)} %copy-done.17), channel_id=1, source_target_pairs={{0,1},{1,2},{2,3},{3,4},{4,5},{5,6},{6,7},{7,0},{8,9},{9,10},{10,1... | collective-permute-start | bytes 786440 | tf_op jit(solution)/shard_map/ppermute | solution.py:321
  117.2 24.9 %collective-permute-start.13 = (bf16[2,128,512]{2,1,0:T(8,128)(2,1)S(1)}, bf16[2,128,512]{2,1,0:T(8,128)(2,1)S(1)}, u32[]{:S(2)}, u32[]{:S(2)}) collective-permute-start(bf16[2,128,512]{2,1,0:T(8,128)(2,1)S(1)} %copy-done.16), channel_id=1, source_target_pairs={{0,7},{1,0},{2,1},{3,2},{4,3},{5,4},{6,5},{7,6},{8,15},{9,8},{10,9... | collective-permute-start | bytes 786440 | tf_op jit(solution)/shard_map/ppermute | solution.py:321
  (9 other events, 21.8 us)
where the time goes:
time: 146 us; the launch traced here: 145 us
  starting transfers between devices  60.3 us (41%)
  waiting for transfers between devices  46.3 us (32%)
  Pallas kernels  27.3 us (19%)
  local copies, waits for them, and re-layouts  5.04 us (3%)
  between operations  4.29 us (3%)
  other arithmetic  2.27 us (2%)
    ppermute x14, waiting for transfers between devices, shifted(): lax.ppermute(arrays[s], 'seq', [(d, (d + s) % seq) for d in range(seq)])  39.3 us
    ppermute x14, starting transfers between devices, shifted(): lax.ppermute(arrays[s], 'seq', [(d, (d + s) % seq) for d in range(seq)])  31.2 us
    pallas_call x5, Pallas kernels, call(): pl.pallas_call(kernel, out_shape=outs, in_specs=[SMEM] + [HBM] * (len(ope...  27.3 us
    all_to_all x2, starting transfers between devices, swapped(): spread = lax.all_to_all(pieces, 'dp', 0, 0, tiled=True)  16.4 us
    all_to_all x2, starting transfers between devices, swapped(): return lax.all_to_all(routed, 'dp', 0, 0, tiled=True).reshape(shape)  12.7 us
    all_to_all x2, waiting for transfers between devices, swapped(): spread = lax.all_to_all(pieces, 'dp', 0, 0, tiled=True)  7.06 us
    unnamed x46, local copies, waits for them, and re-layouts  3.58 us
  transfers between devices with their start and end apart: 18, of which 10 were waited for; matrix products, arithmetic and copies ran while one was open for 3% of the time, Pallas kernels for 3%

commit v1 on v0

--- a/solution.py
+++ b/solution.py
@@ -263,8 +263,11 @@
         sums[1, :, :, cols] = both[:, :, HD:]
     stores.start(sums.at[0], gk)
     stores.start(sums.at[1], gv)
-    loads.wait(seq)
-    stores.start(wide, gq)
+    for s in range(seq):
+        loads.wait(seq + s, seq + s + 1)
+        cols = part(lax.rem(me + seq - s, seq), 256)
+        stores.start(wide.at[:, :, cols], gq.at[:, :, cols])
+    loads.wait(2 * seq)
     stores.start(held, att.at[rows[1]])
     stores.wait()
 
@@ -286,7 +289,7 @@
             pltpu.VMEM((2, 2, tok, KVH * HD), BF16),
             pltpu.VMEM(row.shape, BF16),
             pltpu.SemaphoreType.DMA((2 * seq + 1,)),
-            pltpu.SemaphoreType.DMA((4,)),
+            pltpu.SemaphoreType.DMA((seq + 3,)),
         ],
         "unpack",
         limit=16,

time: 146 us -> 146 us (level)
  no operation moved by 1% of the time
where the time goes in v1:
time: 146 us
  starting transfers between devices  60.3 us (41%)
  waiting for transfers between devices  46.3 us (32%)
  Pallas kernels  27.3 us (19%)
  local copies, waits for them, and re-layouts  5.04 us (3%)
  between operations  4.29 us (3%)
  other arithmetic  2.27 us (2%)
    ppermute x14, waiting for transfers between devices, shifted(): lax.ppermute(arrays[s], 'seq', [(d, (d + s) % seq) for d in range(seq)])  39.3 us
    ppermute x14, starting transfers between devices, shifted(): lax.ppermute(arrays[s], 'seq', [(d, (d + s) % seq) for d in range(seq)])  31.2 us
    pallas_call x5, Pallas kernels, call(): pl.pallas_call(kernel, out_shape=outs, in_specs=[SMEM] + [HBM] * (len(ope...  27.3 us
    all_to_all x2, starting transfers between devices, swapped(): spread = lax.all_to_all(pieces, 'dp', 0, 0, tiled=True)  16.4 us
    all_to_all x2, starting transfers between devices, swapped(): return lax.all_to_all(routed, 'dp', 0, 0, tiled=True).reshape(shape)  12.7 us
    all_to_all x2, waiting for transfers between devices, swapped(): spread = lax.all_to_all(pieces, 'dp', 0, 0, tiled=True)  7.06 us
    unnamed x46, local copies, waits for them, and re-layouts  3.58 us
  transfers between devices with their start and end apart: 18, of which 10 were waited for; matrix products, arithmetic and copies ran while one was open for 3% of the time, Pallas kernels for 3%

profile of v1, /device:TPU:1, one launch (start us, length us, event | category | flops | bytes accessed | tf_op | source)
XLA Modules:
  0.0 145.6 jit_solution(2243058564393247042)
XLA Ops:
  0.6 3.6 %pack.1 = (bf16[2,128,512]{2,1,0:T(8,128)(2,1)}, bf16[2,128,512]{2,1,0:T(8,128)(2,1)}, bf16[2,128,512]{2,1,0:T(8,128)(2,1)}, bf16[2,128,512]{2,1,0:T(8,128)(2,1)...) custom-call(s32[1,32]{1,0:T(1,128)} %bitcast.9, ...), custom_call_target="tpu_custom_call" | custom-call | bytes 2097152 | tf_op jit(solution)/shard_map/pack/pallas_call | solution.py:53
  4.2 8.7 %all-to-all-start = ((bf16[32,32,256]{2,1,0:T(8,128)(2,1)}), bf16[32,32,256]{2,1,0:T(8,128)(2,1)S(1)}, u32[]{:S(2)}, u32[]{:S(2)}) async-start(bf16[32,32,256]{2,1,0:T(8,128)(2,1)} %bitcast.12), calls=%async_computation | async-start | bytes 1048576 | tf_op jit(solution)/shard_map/all_to_all | solution.py:332
  13.0 1.7 %collective-permute-start = (bf16[2,128,512]{2,1,0:T(8,128)(2,1)}, bf16[2,128,512]{2,1,0:T(8,128)(2,1)S(1)}, u32[]{:S(2)}, u32[]{:S(2)}) collective-permute-start(bf16[2,128,512]{2,1,0:T(8,128)(2,1)} %get-tuple-element.24), channel_id=1, source_target_pairs={{0,1},{1,2},{2,3},{3,4},{4,5},{5,6},{6,7},{7,0},{8,9},{9,10},{10,1... | collective-permute-start | bytes 786440 | tf_op jit(solution)/shard_map/ppermute | solution.py:324
  14.7 4.0 %collective-permute-start.1 = (bf16[2,128,512]{2,1,0:T(8,128)(2,1)S(1)}, bf16[2,128,512]{2,1,0:T(8,128)(2,1)S(1)}, u32[]{:S(2)}, u32[]{:S(2)}) collective-permute-start(bf16[2,128,512]{2,1,0:T(8,128)(2,1)S(1)} %copy-done.15), channel_id=1, source_target_pairs={{0,7},{1,0},{2,1},{3,2},{4,3},{5,4},{6,5},{7,6},{8,15},{9,8},{10,9... | collective-permute-start | bytes 786440 | tf_op jit(solution)/shard_map/ppermute | solution.py:324
  18.7 3.9 %collective-permute-start.2 = (bf16[2,128,512]{2,1,0:T(8,128)(2,1)S(1)}, bf16[2,128,512]{2,1,0:T(8,128)(2,1)S(1)}, u32[]{:S(2)}, u32[]{:S(2)}) collective-permute-start(bf16[2,128,512]{2,1,0:T(8,128)(2,1)S(1)} %copy-done.14), channel_id=1, source_target_pairs={{0,4},{1,5},{2,6},{3,7},{4,0},{5,1},{6,2},{7,3},{8,12},{9,13},{10,... | collective-permute-start | bytes 786440 | tf_op jit(solution)/shard_map/ppermute | solution.py:324
  23.1 4.0 %collective-permute-start.4 = (bf16[2,128,512]{2,1,0:T(8,128)(2,1)S(1)}, bf16[2,128,512]{2,1,0:T(8,128)(2,1)S(1)}, u32[]{:S(2)}, u32[]{:S(2)}) collective-permute-start(bf16[2,128,512]{2,1,0:T(8,128)(2,1)S(1)} %copy-done.12), channel_id=1, source_target_pairs={{0,5},{1,6},{2,7},{3,0},{4,1},{5,2},{6,3},{7,4},{8,13},{9,14},{10,... | collective-permute-start | bytes 786440 | tf_op jit(solution)/shard_map/ppermute | solution.py:324
  32.2 2.5 %route.2 = bf16[32,32,256]{2,1,0:T(8,128)(2,1)} custom-call(s32[32]{0:T(128)S(1)} %copy-done.1, bf16[32,32,256]{2,1,0:T(8,128)(2,1)S(1)} %all-to-all-done.spread), custom_call_target="tpu_custom_call" | custom-call | bytes 2097152 | tf_op jit(solution)/shard_map/route/pallas_call | solution.py:53
  34.7 8.9 %all-to-all-start.1 = ((bf16[32,32,256]{2,1,0:T(8,128)(2,1)}), bf16[32,32,256]{2,1,0:T(8,128)(2,1)S(1)}, u32[]{:S(2)}, u32[]{:S(2)}) async-start(bf16[32,32,256]{2,1,0:T(8,128)(2,1)} %route.2), calls=%async_computation.1 | async-start | bytes 1048576 | tf_op jit(solution)/shard_map/all_to_all | solution.py:334
  43.7 0.9 constant_dynamic-slice_fusion
  44.7 3.8 %collective-permute-start.6 = (bf16[2,128,512]{2,1,0:T(8,128)(2,1)S(1)}, bf16[2,128,512]{2,1,0:T(8,128)(2,1)S(1)}, u32[]{:S(2)}, u32[]{:S(2)}) collective-permute-start(bf16[2,128,512]{2,1,0:T(8,128)(2,1)S(1)} %copy-done.10), channel_id=1, source_target_pairs={{0,6},{1,7},{2,0},{3,1},{4,2},{5,3},{6,4},{7,5},{8,14},{9,15},{10,... | collective-permute-start | bytes 786440 | tf_op jit(solution)/shard_map/ppermute | solution.py:324
  48.5 1.1 fusion
  49.6 1.1 select_convert_fusion
  50.8 1.7 %collective-permute-done.3.refs_4_ = bf16[2,128,512]{2,1,0:T(8,128)(2,1)S(1)} collective-permute-done((bf16[2,128,512]{2,1,0:T(8,128)(2,1)S(1)}, bf16[2,128,512]{2,1,0:T(8,128)(2,1)S(1)}, u32[]{:S(2)}, u32[]{:S(2)}) %collective-permute-start.3) | collective-permute-done | bytes 262176 | tf_op jit(solution)/shard_map/ppermute | solution.py:324
  52.5 5.3 %collective-permute-done.4.refs_5_ = bf16[2,128,512]{2,1,0:T(8,128)(2,1)S(1)} collective-permute-done((bf16[2,128,512]{2,1,0:T(8,128)(2,1)S(1)}, bf16[2,128,512]{2,1,0:T(8,128)(2,1)S(1)}, u32[]{:S(2)}, u32[]{:S(2)}) %collective-permute-start.4) | collective-permute-done | bytes 262176 | tf_op jit(solution)/shard_map/ppermute | solution.py:324
  57.8 2.5 %collective-permute-done.5.refs_6_ = bf16[2,128,512]{2,1,0:T(8,128)(2,1)S(1)} collective-permute-done((bf16[2,128,512]{2,1,0:T(8,128)(2,1)S(1)}, bf16[2,128,512]{2,1,0:T(8,128)(2,1)S(1)}, u32[]{:S(2)}, u32[]{:S(2)}) %collective-permute-start.5) | collective-permute-done | bytes 262176 | tf_op jit(solution)/shard_map/ppermute | solution.py:324
  61.0 5.4 %collective-permute-done.6.refs_7_ = bf16[2,128,512]{2,1,0:T(8,128)(2,1)S(1)} collective-permute-done((bf16[2,128,512]{2,1,0:T(8,128)(2,1)S(1)}, bf16[2,128,512]{2,1,0:T(8,128)(2,1)S(1)}, u32[]{:S(2)}, u32[]{:S(2)}) %collective-permute-start.6) | collective-permute-done | bytes 262176 | tf_op jit(solution)/shard_map/ppermute | solution.py:324
  67.2 16.3 %rows.1 = (bf16[2,1024,256]{2,1,0:T(8,128)(2,1)}, bf16[1024,256]{1,0:T(8,128)(2,1)}, bf16[2,128,512]{2,1,0:T(8,128)(2,1)}, bf16[2,128,512]{2,1,0:T(8,128)(2,1)},...) custom-call(s32[1,32]{1,0:T(1,128)} %bitcast.10, ...), custom_call_target="tpu_custom_call" | custom-call | flops 20000000000 | bytes 1048576 | tf_op jit(solution)/shard_map/rows/pallas_call | solution.py:53
  83.5 7.6 %all-to-all-start.2 = ((bf16[32,32,256]{2,1,0:T(8,128)(2,1)}), bf16[32,32,256]{2,1,0:T(8,128)(2,1)S(1)}, u32[]{:S(2)}, u32[]{:S(2)}) async-start(bf16[32,32,256]{2,1,0:T(8,128)(2,1)} %bitcast.14), calls=%async_computation.2 | async-start | bytes 1048576 | tf_op jit(solution)/shard_map/all_to_all | solution.py:332
  91.2 0.8 collective-permute-start.7
  92.0 3.8 %collective-permute-start.8 = (bf16[2,128,512]{2,1,0:T(8,128)(2,1)S(1)}, bf16[2,128,512]{2,1,0:T(8,128)(2,1)S(1)}, u32[]{:S(2)}, u32[]{:S(2)}) collective-permute-start(bf16[2,128,512]{2,1,0:T(8,128)(2,1)S(1)} %copy-done.19), channel_id=1, source_target_pairs={{0,5},{1,6},{2,7},{3,0},{4,1},{5,2},{6,3},{7,4},{8,13},{9,14},{10,... | collective-permute-start | bytes 786440 | tf_op jit(solution)/shard_map/ppermute | solution.py:324
  95.8 7.1 %all-to-all-done.2.spread = bf16[32,32,256]{2,1,0:T(8,128)(2,1)S(1)} async-done(((bf16[32,32,256]{2,1,0:T(8,128)(2,1)}), bf16[32,32,256]{2,1,0:T(8,128)(2,1)S(1)}, u32[]{:S(2)}, u32[]{:S(2)}) %all-to-all-start.2) | async-done | bytes 524320 | tf_op jit(solution)/shard_map/all_to_all | solution.py:332
  102.8 2.5 %route.3 = bf16[32,32,256]{2,1,0:T(8,128)(2,1)} custom-call(s32[32]{0:T(128)S(1)} %copy-done.1, bf16[32,32,256]{2,1,0:T(8,128)(2,1)S(1)} %all-to-all-done.2.spread), custom_call_target="tpu_custom_call" | custom-call | bytes 2097152 | tf_op jit(solution)/shard_map/route/pallas_call | solution.py:53
  105.3 3.8 %all-to-all-start.3 = ((bf16[32,32,256]{2,1,0:T(8,128)(2,1)}), bf16[32,32,256]{2,1,0:T(8,128)(2,1)S(1)}, u32[]{:S(2)}, u32[]{:S(2)}) async-start(bf16[32,32,256]{2,1,0:T(8,128)(2,1)} %route.3), calls=%async_computation.3 | async-start | bytes 1048576 | tf_op jit(solution)/shard_map/all_to_all | solution.py:334
  109.2 2.5 %collective-permute-start.9 = (bf16[2,128,512]{2,1,0:T(8,128)(2,1)}, bf16[2,128,512]{2,1,0:T(8,128)(2,1)S(1)}, u32[]{:S(2)}, u32[]{:S(2)}) collective-permute-start(bf16[2,128,512]{2,1,0:T(8,128)(2,1)} %get-tuple-element.35), channel_id=1, source_target_pairs={{0,2},{1,3},{2,4},{3,5},{4,6},{5,7},{6,0},{7,1},{8,10},{9,11},{10,... | collective-permute-start | bytes 786440 | tf_op jit(solution)/shard_map/ppermute | solution.py:324
  111.7 1.1 collective-permute-start.10
  112.8 2.3 %collective-permute-start.11 = (bf16[2,128,512]{2,1,0:T(8,128)(2,1)S(1)}, bf16[2,128,512]{2,1,0:T(8,128)(2,1)S(1)}, u32[]{:S(2)}, u32[]{:S(2)}) collective-permute-start(bf16[2,128,512]{2,1,0:T(8,128)(2,1)S(1)} %copy-done.18), channel_id=1, source_target_pairs={{0,4},{1,5},{2,6},{3,7},{4,0},{5,1},{6,2},{7,3},{8,12},{9,13},{10,... | collective-permute-start | bytes 786440 | tf_op jit(solution)/shard_map/ppermute | solution.py:324
  115.1 2.2 %collective-permute-start.12 = (bf16[2,128,512]{2,1,0:T(8,128)(2,1)S(1)}, bf16[2,128,512]{2,1,0:T(8,128)(2,1)S(1)}, u32[]{:S(2)}, u32[]{:S(2)}) collective-permute-start(bf16[2,128,512]{2,1,0:T(8,128)(2,1)S(1)} %copy-done.17), channel_id=1, source_target_pairs={{0,1},{1,2},{2,3},{3,4},{4,5},{5,6},{6,7},{7,0},{8,9},{9,10},{10,1... | collective-permute-start | bytes 786440 | tf_op jit(solution)/shard_map/ppermute | solution.py:324
  117.8 6.9 %collective-permute-done.9.refs_3_ = bf16[2,128,512]{2,1,0:T(8,128)(2,1)S(1)} collective-permute-done((bf16[2,128,512]{2,1,0:T(8,128)(2,1)}, bf16[2,128,512]{2,1,0:T(8,128)(2,1)S(1)}, u32[]{:S(2)}, u32[]{:S(2)}) %collective-permute-start.9) | collective-permute-done | bytes 262176 | tf_op jit(solution)/shard_map/ppermute | solution.py:324
  124.7 1.8 %collective-permute-done.10.refs_4_ = bf16[2,128,512]{2,1,0:T(8,128)(2,1)S(1)} collective-permute-done((bf16[2,128,512]{2,1,0:T(8,128)(2,1)}, bf16[2,128,512]{2,1,0:T(8,128)(2,1)S(1)}, u32[]{:S(2)}, u32[]{:S(2)}) %collective-permute-start.10) | collective-permute-done | bytes 262176 | tf_op jit(solution)/shard_map/ppermute | solution.py:324
  126.5 11.6 %collective-permute-done.11.refs_5_ = bf16[2,128,512]{2,1,0:T(8,128)(2,1)S(1)} collective-permute-done((bf16[2,128,512]{2,1,0:T(8,128)(2,1)S(1)}, bf16[2,128,512]{2,1,0:T(8,128)(2,1)S(1)}, u32[]{:S(2)}, u32[]{:S(2)}) %collective-permute-start.11) | collective-permute-done | bytes 262176 | tf_op jit(solution)/shard_map/ppermute | solution.py:324
  138.1 3.3 %collective-permute-done.12.refs_6_ = bf16[2,128,512]{2,1,0:T(8,128)(2,1)S(1)} collective-permute-done((bf16[2,128,512]{2,1,0:T(8,128)(2,1)S(1)}, bf16[2,128,512]{2,1,0:T(8,128)(2,1)S(1)}, u32[]{:S(2)}, u32[]{:S(2)}) %collective-permute-start.12) | collective-permute-done | bytes 262176 | tf_op jit(solution)/shard_map/ppermute | solution.py:324
  142.8 2.5 %unpack.1 = (bf16[2,1024,256]{2,1,0:T(8,128)(2,1)}, bf16[2,128,2048]{2,1,0:T(8,128)(2,1)}, bf16[2,128,512]{2,1,0:T(8,128)(2,1)}, bf16[2,128,512]{2,1,0:T(8,128)(2,1)}) custom-call(s32[1,32]{1,0:T(1,128)S(1)} %bitcast.11, bf16[2,128,512]{2,1,0:T(8,128)(2,1)S(1)} %copy-done, ...), custom_call_target="tpu_custom_call", output_to_operand_aliasing={{0}: (10, {})} | custom-call | bytes 2097152 | tf_op jit(solution)/shard_map/unpack/pallas_call | solution.py:53
  (59 shorter events, 6.0 us)
Async XLA Ops:
  4.2 10.5 %copy-start.15 = (bf16[2,128,512]{2,1,0:T(8,128)(2,1)S(1)}, bf16[2,128,512]{2,1,0:T(8,128)(2,1)}, u32[]{:S(2)}) copy-start(bf16[2,128,512]{2,1,0:T(8,128)(2,1)} %get-tuple-element.25) | copy-start | bytes 786436
  4.2 14.5 %copy-start.14 = (bf16[2,128,512]{2,1,0:T(8,128)(2,1)S(1)}, bf16[2,128,512]{2,1,0:T(8,128)(2,1)}, u32[]{:S(2)}) copy-start(bf16[2,128,512]{2,1,0:T(8,128)(2,1)} %get-tuple-element.26) | copy-start | bytes 786436
  4.2 18.4 %copy-start.13 = (bf16[2,128,512]{2,1,0:T(8,128)(2,1)S(1)}, bf16[2,128,512]{2,1,0:T(8,128)(2,1)}, u32[]{:S(2)}) copy-start(bf16[2,128,512]{2,1,0:T(8,128)(2,1)} %get-tuple-element.27) | copy-start | bytes 786436
  4.2 18.9 %copy-start.12 = (bf16[2,128,512]{2,1,0:T(8,128)(2,1)S(1)}, bf16[2,128,512]{2,1,0:T(8,128)(2,1)}, u32[]{:S(2)}) copy-start(bf16[2,128,512]{2,1,0:T(8,128)(2,1)} %get-tuple-element.28) | copy-start | bytes 786436
  4.2 27.4 %all-to-all-start = ((bf16[32,32,256]{2,1,0:T(8,128)(2,1)}), bf16[32,32,256]{2,1,0:T(8,128)(2,1)S(1)}, u32[]{:S(2)}, u32[]{:S(2)}) async-start(bf16[32,32,256]{2,1,0:T(8,128)(2,1)} %bitcast.12), calls=%async_computation | async-start | bytes 1048576 | tf_op jit(solution)/shard_map/all_to_all | solution.py:332
  13.0 31.5 %collective-permute-start = (bf16[2,128,512]{2,1,0:T(8,128)(2,1)}, bf16[2,128,512]{2,1,0:T(8,128)(2,1)S(1)}, u32[]{:S(2)}, u32[]{:S(2)}) collective-permute-start(bf16[2,128,512]{2,1,0:T(8,128)(2,1)} %get-tuple-element.24), channel_id=1, source_target_pairs={{0,1},{1,2},{2,3},{3,4},{4,5},{5,6},{6,7},{7,0},{8,9},{9,10},{10,1... | collective-permute-start | bytes 786440 | tf_op jit(solution)/shard_map/ppermute | solution.py:324
  14.7 30.0 %collective-permute-start.1 = (bf16[2,128,512]{2,1,0:T(8,128)(2,1)S(1)}, bf16[2,128,512]{2,1,0:T(8,128)(2,1)S(1)}, u32[]{:S(2)}, u32[]{:S(2)}) collective-permute-start(bf16[2,128,512]{2,1,0:T(8,128)(2,1)S(1)} %copy-done.15), channel_id=1, source_target_pairs={{0,7},{1,0},{2,1},{3,2},{4,3},{5,4},{6,5},{7,6},{8,15},{9,8},{10,9... | collective-permute-start | bytes 786440 | tf_op jit(solution)/shard_map/ppermute | solution.py:324
  18.7 32.0 %collective-permute-start.2 = (bf16[2,128,512]{2,1,0:T(8,128)(2,1)S(1)}, bf16[2,128,512]{2,1,0:T(8,128)(2,1)S(1)}, u32[]{:S(2)}, u32[]{:S(2)}) collective-permute-start(bf16[2,128,512]{2,1,0:T(8,128)(2,1)S(1)} %copy-done.14), channel_id=1, source_target_pairs={{0,4},{1,5},{2,6},{3,7},{4,0},{5,1},{6,2},{7,3},{8,12},{9,13},{10,... | collective-permute-start | bytes 786440 | tf_op jit(solution)/shard_map/ppermute | solution.py:324
  22.7 29.8 %collective-permute-start.3 = (bf16[2,128,512]{2,1,0:T(8,128)(2,1)S(1)}, bf16[2,128,512]{2,1,0:T(8,128)(2,1)S(1)}, u32[]{:S(2)}, u32[]{:S(2)}) collective-permute-start(bf16[2,128,512]{2,1,0:T(8,128)(2,1)S(1)} %copy-done.13), channel_id=1, source_target_pairs={{0,3},{1,4},{2,5},{3,6},{4,7},{5,0},{6,1},{7,2},{8,11},{9,12},{10,... | collective-permute-start | bytes 786440 | tf_op jit(solution)/shard_map/ppermute | solution.py:324
  23.1 34.7 %collective-permute-start.4 = (bf16[2,128,512]{2,1,0:T(8,128)(2,1)S(1)}, bf16[2,128,512]{2,1,0:T(8,128)(2,1)S(1)}, u32[]{:S(2)}, u32[]{:S(2)}) collective-permute-start(bf16[2,128,512]{2,1,0:T(8,128)(2,1)S(1)} %copy-done.12), channel_id=1, source_target_pairs={{0,5},{1,6},{2,7},{3,0},{4,1},{5,2},{6,3},{7,4},{8,13},{9,14},{10,... | collective-permute-start | bytes 786440 | tf_op jit(solution)/shard_map/ppermute | solution.py:324
  34.7 9.8 %copy-start.11 = (bf16[2,128,512]{2,1,0:T(8,128)(2,1)S(1)}, bf16[2,128,512]{2,1,0:T(8,128)(2,1)}, u32[]{:S(2)}) copy-start(bf16[2,128,512]{2,1,0:T(8,128)(2,1)} %get-tuple-element.29) | copy-start | bytes 786436
  34.7 9.9 %copy-start.10 = (bf16[2,128,512]{2,1,0:T(8,128)(2,1)S(1)}, bf16[2,128,512]{2,1,0:T(8,128)(2,1)}, u32[]{:S(2)}) copy-start(bf16[2,128,512]{2,1,0:T(8,128)(2,1)} %get-tuple-element.30) | copy-start | bytes 786436
  34.7 31.6 %all-to-all-start.1 = ((bf16[32,32,256]{2,1,0:T(8,128)(2,1)}), bf16[32,32,256]{2,1,0:T(8,128)(2,1)S(1)}, u32[]{:S(2)}, u32[]{:S(2)}) async-start(bf16[32,32,256]{2,1,0:T(8,128)(2,1)} %route.2), calls=%async_computation.1 | async-start | bytes 1048576 | tf_op jit(solution)/shard_map/all_to_all | solution.py:334
  44.6 15.7 %collective-permute-start.5 = (bf16[2,128,512]{2,1,0:T(8,128)(2,1)S(1)}, bf16[2,128,512]{2,1,0:T(8,128)(2,1)S(1)}, u32[]{:S(2)}, u32[]{:S(2)}) collective-permute-start(bf16[2,128,512]{2,1,0:T(8,128)(2,1)S(1)} %copy-done.11), channel_id=1, source_target_pairs={{0,2},{1,3},{2,4},{3,5},{4,6},{5,7},{6,0},{7,1},{8,10},{9,11},{10,... | collective-permute-start | bytes 786440 | tf_op jit(solution)/shard_map/ppermute | solution.py:324
  44.7 21.7 %collective-permute-start.6 = (bf16[2,128,512]{2,1,0:T(8,128)(2,1)S(1)}, bf16[2,128,512]{2,1,0:T(8,128)(2,1)S(1)}, u32[]{:S(2)}, u32[]{:S(2)}) collective-permute-start(bf16[2,128,512]{2,1,0:T(8,128)(2,1)S(1)} %copy-done.10), channel_id=1, source_target_pairs={{0,6},{1,7},{2,0},{3,1},{4,2},{5,3},{6,4},{7,5},{8,14},{9,15},{10,... | collective-permute-start | bytes 786440 | tf_op jit(solution)/shard_map/ppermute | solution.py:324
  50.8 15.6 %copy-start.7 = (bf16[2,128,512]{2,1,0:T(8,128)(2,1)}, bf16[2,128,512]{2,1,0:T(8,128)(2,1)S(1)}, u32[]{:S(2)}) copy-start(bf16[2,128,512]{2,1,0:T(8,128)(2,1)S(1)} %collective-permute-done.2.refs_3_) | copy-start | bytes 786436
  52.5 13.9 %copy-start.8 = (bf16[2,128,512]{2,1,0:T(8,128)(2,1)}, bf16[2,128,512]{2,1,0:T(8,128)(2,1)S(1)}, u32[]{:S(2)}) copy-start(bf16[2,128,512]{2,1,0:T(8,128)(2,1)S(1)} %collective-permute-done.3.refs_4_) | copy-start | bytes 786436
  57.8 8.6 %copy-start.9 = (bf16[2,128,512]{2,1,0:T(8,128)(2,1)}, bf16[2,128,512]{2,1,0:T(8,128)(2,1)S(1)}, u32[]{:S(2)}) copy-start(bf16[2,128,512]{2,1,0:T(8,128)(2,1)S(1)} %collective-permute-done.4.refs_5_) | copy-start | bytes 786436
  83.5 7.7 %copy-start.21 = (bf16[2,128,512]{2,1,0:T(8,128)(2,1)S(1)}, bf16[2,128,512]{2,1,0:T(8,128)(2,1)}, u32[]{:S(2)}) copy-start(bf16[2,128,512]{2,1,0:T(8,128)(2,1)} %get-tuple-element.33) | copy-start | bytes 786436
  83.5 8.4 %copy-start.19 = (bf16[2,128,512]{2,1,0:T(8,128)(2,1)S(1)}, bf16[2,128,512]{2,1,0:T(8,128)(2,1)}, u32[]{:S(2)}) copy-start(bf16[2,128,512]{2,1,0:T(8,128)(2,1)} %get-tuple-element.34) | copy-start | bytes 786436
  83.5 19.3 %all-to-all-start.2 = ((bf16[32,32,256]{2,1,0:T(8,128)(2,1)}), bf16[32,32,256]{2,1,0:T(8,128)(2,1)S(1)}, u32[]{:S(2)}, u32[]{:S(2)}) async-start(bf16[32,32,256]{2,1,0:T(8,128)(2,1)} %bitcast.14), calls=%async_computation.2 | async-start | bytes 1048576 | tf_op jit(solution)/shard_map/all_to_all | solution.py:332
  91.2 23.9 %collective-permute-start.7 = (bf16[2,128,512]{2,1,0:T(8,128)(2,1)S(1)}, bf16[2,128,512]{2,1,0:T(8,128)(2,1)S(1)}, u32[]{:S(2)}, u32[]{:S(2)}) collective-permute-start(bf16[2,128,512]{2,1,0:T(8,128)(2,1)S(1)} %copy-done.21), channel_id=1, source_target_pairs={{0,3},{1,4},{2,5},{3,6},{4,7},{5,0},{6,1},{7,2},{8,11},{9,12},{10,... | collective-permute-start | bytes 786440 | tf_op jit(solution)/shard_map/ppermute | solution.py:324
  92.0 25.3 %collective-permute-start.8 = (bf16[2,128,512]{2,1,0:T(8,128)(2,1)S(1)}, bf16[2,128,512]{2,1,0:T(8,128)(2,1)S(1)}, u32[]{:S(2)}, u32[]{:S(2)}) collective-permute-start(bf16[2,128,512]{2,1,0:T(8,128)(2,1)S(1)} %copy-done.19), channel_id=1, source_target_pairs={{0,5},{1,6},{2,7},{3,0},{4,1},{5,2},{6,3},{7,4},{8,13},{9,14},{10,... | collective-permute-start | bytes 786440 | tf_op jit(solution)/shard_map/ppermute | solution.py:324
  105.3 9.8 %copy-start.17 = (bf16[2,128,512]{2,1,0:T(8,128)(2,1)S(1)}, bf16[2,128,512]{2,1,0:T(8,128)(2,1)}, u32[]{:S(2)}) copy-start(bf16[2,128,512]{2,1,0:T(8,128)(2,1)} %get-tuple-element.38) | copy-start | bytes 786436
  105.3 11.9 %copy-start.16 = (bf16[2,128,512]{2,1,0:T(8,128)(2,1)S(1)}, bf16[2,128,512]{2,1,0:T(8,128)(2,1)}, u32[]{:S(2)}) copy-start(bf16[2,128,512]{2,1,0:T(8,128)(2,1)} %get-tuple-element.39) | copy-start | bytes 786436
  105.3 36.9 %copy-start = (bf16[2,128,512]{2,1,0:T(8,128)(2,1)S(1)}, bf16[2,128,512]{2,1,0:T(8,128)(2,1)}, u32[]{:S(2)}) copy-start(bf16[2,128,512]{2,1,0:T(8,128)(2,1)} %get-tuple-element.32.refs_0_) | copy-start | bytes 786436
  105.3 36.9 %all-to-all-start.3 = ((bf16[32,32,256]{2,1,0:T(8,128)(2,1)}), bf16[32,32,256]{2,1,0:T(8,128)(2,1)S(1)}, u32[]{:S(2)}, u32[]{:S(2)}) async-start(bf16[32,32,256]{2,1,0:T(8,128)(2,1)} %route.3), calls=%async_computation.3 | async-start | bytes 1048576 | tf_op jit(solution)/shard_map/all_to_all | solution.py:334
  109.2 15.5 %collective-permute-start.9 = (bf16[2,128,512]{2,1,0:T(8,128)(2,1)}, bf16[2,128,512]{2,1,0:T(8,128)(2,1)S(1)}, u32[]{:S(2)}, u32[]{:S(2)}) collective-permute-start(bf16[2,128,512]{2,1,0:T(8,128)(2,1)} %get-tuple-element.35), channel_id=1, source_target_pairs={{0,2},{1,3},{2,4},{3,5},{4,6},{5,7},{6,0},{7,1},{8,10},{9,11},{10,... | collective-permute-start | bytes 786440 | tf_op jit(solution)/shard_map/ppermute | solution.py:324
  111.7 14.8 %collective-permute-start.10 = (bf16[2,128,512]{2,1,0:T(8,128)(2,1)}, bf16[2,128,512]{2,1,0:T(8,128)(2,1)S(1)}, u32[]{:S(2)}, u32[]{:S(2)}) collective-permute-start(bf16[2,128,512]{2,1,0:T(8,128)(2,1)} %get-tuple-element.36), channel_id=1, source_target_pairs={{0,6},{1,7},{2,0},{3,1},{4,2},{5,3},{6,4},{7,5},{8,14},{9,15},{10,... | collective-permute-start | bytes 786440 | tf_op jit(solution)/shard_map/ppermute | solution.py:324
  112.8 25.3 %collective-permute-start.11 = (bf16[2,128,512]{2,1,0:T(8,128)(2,1)S(1)}, bf16[2,128,512]{2,1,0:T(8,128)(2,1)S(1)}, u32[]{:S(2)}, u32[]{:S(2)}) collective-permute-start(bf16[2,128,512]{2,1,0:T(8,128)(2,1)S(1)} %copy-done.18), channel_id=1, source_target_pairs={{0,4},{1,5},{2,6},{3,7},{4,0},{5,1},{6,2},{7,3},{8,12},{9,13},{10,... | collective-permute-start | bytes 786440 | tf_op jit(solution)/shard_map/ppermute | solution.py:324
  115.1 26.3 %collective-permute-start.12 = (bf16[2,128,512]{2,1,0:T(8,128)(2,1)S(1)}, bf16[2,128,512]{2,1,0:T(8,128)(2,1)S(1)}, u32[]{:S(2)}, u32[]{:S(2)}) collective-permute-start(bf16[2,128,512]{2,1,0:T(8,128)(2,1)S(1)} %copy-done.17), channel_id=1, source_target_pairs={{0,1},{1,2},{2,3},{3,4},{4,5},{5,6},{6,7},{7,0},{8,9},{9,10},{10,1... | collective-permute-start | bytes 786440 | tf_op jit(solution)/shard_map/ppermute | solution.py:324
  117.3 24.9 %collective-permute-start.13 = (bf16[2,128,512]{2,1,0:T(8,128)(2,1)S(1)}, bf16[2,128,512]{2,1,0:T(8,128)(2,1)S(1)}, u32[]{:S(2)}, u32[]{:S(2)}) collective-permute-start(bf16[2,128,512]{2,1,0:T(8,128)(2,1)S(1)} %copy-done.16), channel_id=1, source_target_pairs={{0,7},{1,0},{2,1},{3,2},{4,3},{5,4},{6,5},{7,6},{8,15},{9,8},{10,9... | collective-permute-start | bytes 786440 | tf_op jit(solution)/shard_map/ppermute | solution.py:324
  (9 other events, 21.8 us)
